TPU v7x, 32 devices: a whole 2x2x4 slice. The times are simulated.
32 devices in a mesh: grp: 2 (over x), wide: 16 (over z, y, core).
Axes of the slice: x: 2, y: 2, z: 4, core: 2. Of those that a mesh axis runs over, the one named last changes fastest.
Arguments:
- voltages: bfloat16 [2048, 131, 2048], P(('grp', 'wide')), parts along dimension 0, may hold values from -6 to 6
- filter_taps: bfloat16 [4, 2048], replicated, may hold values from -3 to 3
- input_gain: float32 [2048], P(('grp', 'wide')), parts along dimension 0, may hold values from 0.5 to 11, as said below
- input_flags: int32 [2048], P(('grp', 'wide')), parts along dimension 0, may hold values 0 or 1
- kept_channels: int32 [256], replicated, may hold values from 0 to 1023, as said below
- tile_order: int32 [10], replicated, may hold values from 0 to 9, each once
Outputs:
- visibilities: bfloat16 [512, 10, 2, 256, 256], P(('grp', 'wide')), parts along dimension 0
There are 2 independent parts, one for each index of `grp`. A program takes and returns all parts, laid end to end along the dimension named above; an argument that names none is the same for every part. Nothing has to cross between parts.
Inputs may be any that keep to these rules, and one draw needn't show every extreme that they name: `kept_channels`: the 256 channel numbers are distinct; channels 0 and 1023 are always among them. `tile_order`: each tile number appears once. `input_gain`: gains are positive.
All inputs are finite; a program needn't handle non-finite values. No bound on the sum of `input_flags` on one device may be relied on, other than what follows from the above.
Results may differ from a plain program's by a relative error of at most 0.007.
Values may be sent and summed in bfloat16 or wider, within the bound.
A program may use at most 448 MiB of HBM per device.

v0:
```python
import math

import jax
import jax.numpy as jnp
import numpy as np
from jax import lax
from jax.sharding import PartitionSpec as P

BLK = 256


eps_power = 1e-06


def tile_tables(blocks):
    row_list = []
    col_list = []
    for row_block in range(blocks):
        for col_block in range(row_block, blocks):
            row_list.append(row_block)
            col_list.append(col_block)
    return (np.array(row_list, np.int32), np.array(col_list, np.int32))


def dft_table(kept_channels, samples):
    sample_index = jnp.arange(samples, dtype=jnp.int32)
    product = sample_index[:, None] * kept_channels[None, :] % samples
    phase = product.astype(jnp.float32) * jnp.float32(2.0 * math.pi / samples)
    factor = jnp.float32(1.0 / math.sqrt(samples / 2))
    return jnp.concatenate([jnp.cos(phase) * factor, -jnp.sin(phase) * factor], axis=1).astype(
        jnp.bfloat16
    )


def tile_corner(tile_order, slot_index, corner_table):
    picked = tile_order[slot_index] == jnp.arange(corner_table.shape[0], dtype=jnp.int32)
    return jnp.sum(jnp.where(picked, jnp.asarray(corner_table), 0)).astype(jnp.int32)


def visibility_terms(turned, tile_order, block_size):
    real_part = turned[:, 0]
    imag_part = turned[:, 1]
    stacked = jnp.concatenate([real_part, imag_part], axis=1)
    rotated = jnp.concatenate([imag_part, -real_part], axis=1)
    local_channels = turned.shape[0]
    row_table, col_table = tile_tables(turned.shape[3] // block_size)
    tile_list = []
    real_full = jnp.einsum("cfi,cfj->cij", stacked, stacked, preferred_element_type=jnp.float32)
    imag_full = jnp.einsum("cfi,cfj->cij", rotated, stacked, preferred_element_type=jnp.float32)
    for slot_index in range(row_table.shape[0]):
        row_start = tile_corner(tile_order, slot_index, row_table) * block_size
        col_start = tile_corner(tile_order, slot_index, col_table) * block_size
        zero_start = jnp.zeros((), jnp.int32)
        real_tile = lax.dynamic_slice(
            real_full, (zero_start, row_start, col_start), (local_channels, block_size, block_size)
        )
        imag_tile = lax.dynamic_slice(
            imag_full, (zero_start, row_start, col_start), (local_channels, block_size, block_size)
        )
        tile_list.append(jnp.stack([real_tile, imag_tile], axis=1))
    return jnp.stack(tile_list, axis=1)


def body(voltages, filter_taps, input_gain, input_flags, kept_channels, tile_order):
    local_inputs, padded_frames, samples = voltages.shape
    tap_count = filter_taps.shape[0]
    frames = padded_frames - tap_count + 1
    kept = kept_channels.shape[0]
    table = dft_table(kept_channels, samples)
    filtered = jnp.zeros((local_inputs, frames, samples), jnp.float32)
    for tap_index in range(tap_count):
        filtered = filtered + voltages[:, tap_index : tap_index + frames, :].astype(
            jnp.float32
        ) * filter_taps[tap_index].astype(jnp.float32)
    filtered = (filtered * input_gain[:, None, None]).astype(jnp.bfloat16)
    spectra = jnp.dot(
        filtered.reshape(local_inputs * frames, samples), table, preferred_element_type=jnp.float32
    )
    weights = jnp.repeat(input_flags.astype(jnp.float32), frames)[:, None]
    spectra = spectra * weights
    squares = spectra[:, :kept] * spectra[:, :kept] + spectra[:, kept:] * spectra[:, kept:]
    total_power = lax.psum(jnp.sum(squares, axis=0), "wide")
    all_inputs = local_inputs * lax.axis_size("wide")
    power = total_power / jnp.float32(all_inputs * frames) + jnp.float32(eps_power)
    scale = lax.rsqrt(power)
    equalized = (spectra * jnp.concatenate([scale, scale])[None, :]).astype(jnp.bfloat16)
    arranged = equalized.reshape(local_inputs, frames, 2, kept).transpose(3, 2, 1, 0)
    turned = lax.all_to_all(arranged, "wide", split_axis=0, concat_axis=3, tiled=True)
    summed = visibility_terms(turned, tile_order, BLK)
    return (summed * jnp.float32(1.0 / frames)).astype(jnp.bfloat16)


def solution(mesh):
    return jax.shard_map(
        body,
        mesh=mesh,
        in_specs=(
            P(("grp", "wide"), None, None),
            P(),
            P(("grp", "wide")),
            P(("grp", "wide")),
            P(),
            P(),
        ),
        out_specs=P(("grp", "wide"), None, None, None, None),
        check_vma=False,
    )
```

profile of v0, /device:TPU:15, one launch (start us, length us, event | category | flops | bytes accessed | tf_op | source)
XLA Modules:
  0.0 764.7 jit_solution(17555352924429036793)
XLA Ops:
  1.6 9.4 %multiply_convert_fusion.4 = (bf16[2048,256]{1,0:T(8,128)(2,1)S(1)}, bf16[2048,256]{1,0:T(8,128)(2,1)S(1)}) fusion(s32[256]{0:T(256)} %param.12), kind=kLoop, calls=%fused_computation.64 | loop fusion | flops 9961472 | bytes 2098176 | tf_op jit(solution)/shard_map/convert.4
  11.1 86.5 %fusion.49 = (bf16[64,128,2048]{2,0,1:T(8,128)(2,1)}, bf16[64,128,2048]{2,0,1:T(8,128)(2,1)}, bf16[64,128,2048]{2,0,1:T(8,128)(2,1)}, bf16[64,128,2048]{2,0,1:T(8,128)(2,1)}) fusion(bf16[64,131,2048]{2,0,1:T(8,128)(2,1)} %param.8), kind=kLoop, calls=%fused_computation.119 | loop fusion | bytes 268435456 | tf_op jit(solution)/shard_map/slice | solution.py:72
  97.6 119.8 %multiply_convert_fusion.1 = bf16[64,128,2048]{2,1,0:T(8,128)(2,1)} fusion(bf16[64,128,2048]{2,0,1:T(8,128)(2,1)} %get-tuple-element.46, bf16[64,128,2048]{2,0,1:T(8,128)(2,1)} %get-tuple-element.44, bf16[64,128,2048]{2,0,1:T(8,128)(2,1)} %get-tuple-element.45, bf16[64,128,2048]{2,0,1:T(8,128)(2,1)} %get-tuple-element.43, f32[64]{0:T(128)S(1)} %copy-done.21, ...), kind=kLoop, calls=%fused_computation.1 | loop fusion | flops 218103808 | bytes 167805184 | tf_op jit(solution)/shard_map/convert_element_type | solution.py:75
  217.4 25.8 %convolution_multiply_fusion = f32[8192,512]{1,0:T(8,128)} fusion(bf16[8192,2048]{1,0:T(8,128)(2,1)} %bitcast.112, f32[8192]{0:T(1024)S(1)} %broadcast_bitcast_fusion, bf16[2048,256]{1,0:T(8,128)(2,1)S(1)} %get-tuple-element.54, bf16[2048,256]{1,0:T(8,128)(2,1)S(1)} %get-tuple-element.53), kind=kOutput, calls=%fused_computation.3 | convolution fusion | flops 17188257792 | bytes 52461568 | tf_op jit(solution)/shard_map/dot_general | solution.py:76
  243.2 7.0 fusion.1
  250.2 21.8 %psum.7 = f32[256]{0:T(256)S(1)} all-reduce(f32[256]{0:T(256)S(1)} %fusion.1), channel_id=1, replica_groups=mesh['grp'=2,'wide'=16] {'wide'}, use_global_device_ids=true, to_apply=%region_1.2 | all-reduce | flops 256 | bytes 2048 | tf_op jit(solution)/shard_map/psum | solution.py:82
  272.0 9.0 %multiply_convert_fusion.2 = bf16[8192,512]{1,0:T(8,128)(2,1)} fusion(f32[8192,512]{1,0:T(8,128)} %convolution_multiply_fusion, f32[512]{0:T(512)S(1)} %pad_maximum_fusion.3), kind=kLoop, calls=%fused_computation.2 | loop fusion | flops 8388608 | bytes 25167872 | tf_op jit(solution)/shard_map/convert_element_type | solution.py:86
  281.0 12.5 %reshape.39 = bf16[64,128,2,256]{3,2,1,0:T(2,128)(2,1)} reshape(bf16[8192,512]{1,0:T(8,128)(2,1)} %multiply_convert_fusion.2) | data formatting | bytes 16777216 | tf_op jit(solution)/shard_map/reshape | solution.py:87
  293.5 15.5 %copy.16 = bf16[64,128,2,256]{1,0,2,3:T(8,128)(2,1)} copy(bf16[64,128,2,256]{3,2,1,0:T(2,128)(2,1)} %reshape.39) | data formatting | bytes 16777216 | tf_op jit(solution)/shard_map/reshape | solution.py:87
  308.9 17.4 %all-to-all-start = ((bf16[256,2,128,64]{2,3,1,0:T(8,128)(2,1)}), bf16[256,2,128,64]{2,3,1,0:T(8,128)(2,1)}, u32[]{:S(2)}, u32[]{:S(2)}) async-start(bf16[256,2,128,64]{2,3,1,0:T(8,128)(2,1)} %bitcast.110), calls=%async_computation | async-start | bytes 16777216 | tf_op jit(solution)/shard_map/all_to_all | solution.py:88
  327.0 7.3 fusion.44
  346.9 161.6 %all-to-all-done = bf16[256,2,128,64]{2,3,1,0:T(8,128)(2,1)} async-done(((bf16[256,2,128,64]{2,3,1,0:T(8,128)(2,1)}), bf16[256,2,128,64]{2,3,1,0:T(8,128)(2,1)}, u32[]{:S(2)}, u32[]{:S(2)}) %all-to-all-start) | async-done | bytes 8388640 | tf_op jit(solution)/shard_map/all_to_all | solution.py:88
  508.5 9.8 %copy.17 = bf16[16,2,128,16,64]{2,4,3,1,0:T(8,128)(2,1)} copy(bf16[16,2,128,16,64]{2,4,1,0,3:T(8,128)(2,1)} %bitcast.8) | data formatting | bytes 16777216 | tf_op jit(solution)/shard_map/all_to_all | solution.py:88
  518.3 5.9 fusion.50
  524.2 6.4 copy.29
  530.6 6.4 copy.28
  537.0 4.4 bitcast_negate_fusion
  541.4 29.5 %fusion.16 = f32[16,1024,1024]{2,1,0:T(8,128)} fusion(bf16[16,128,1024]{2,1,0:T(8,128)(2,1)} %bitcast.106, bf16[16,128,1024]{2,1,0:T(8,128)(2,1)} %bitcast.108), kind=kOutput, calls=%fused_computation.33 | convolution fusion | flops 8606711808 | bytes 75497472 | tf_op jit(solution)/shard_map/cfi,cfj->cij/dot_general | solution.py:48
  570.9 29.5 %fusion.2 = f32[16,1024,1024]{2,1,0:T(8,128)} fusion(bf16[16,128,1024]{2,1,0:T(8,128)(2,1)} %bitcast_negate_fusion, bf16[16,128,1024]{2,1,0:T(8,128)(2,1)} %bitcast.107, bf16[16,128,1024]{2,1,0:T(8,128)(2,1)} %bitcast.109), kind=kOutput, calls=%fused_computation.9 | convolution fusion | flops 8623489024 | bytes 79691776 | tf_op jit(solution)/shard_map/cfi,cfj->cij/dot_general | solution.py:49
  602.9 4.6 dynamic-slice_bitcast_fusion.19
  607.6 26.8 %dynamic-slice_bitcast_fusion = (f32[16,1,256,256]{3,2,1,0:T(8,128)}, f32[16,1,256,256]{3,2,1,0:T(8,128)}, f32[16,1,256,256]{3,2,1,0:T(8,128)}, f32[16,1,256,256...) fusion(f32[16,1024,1024]{2,1,0:T(8,128)} %fusion.2, ...), kind=kLoop, calls=%fused_computation.34 | loop fusion | bytes 75497544 | tf_op jit(solution)/shard_map/stack | solution.py:60
  634.4 27.0 %dynamic-slice_bitcast_fusion.1 = (f32[16,1,256,256]{3,2,1,0:T(8,128)}, f32[16,1,256,256]{3,2,1,0:T(8,128)}, f32[16,1,256,256]{3,2,1,0:T(8,128)}, f32[16,1,256,2...) fusion(f32[16,1024,1024]{2,1,0:T(8,128)} %fusion.16, ...), kind=kLoop, calls=%fused_computation.35 | loop fusion | bytes 75497544 | tf_op jit(solution)/shard_map/stack | solution.py:60
  661.4 6.6 fusion.6
  668.0 4.8 fusion.7
  674.5 4.8 fusion.8
  681.0 4.8 fusion.9
  687.5 4.8 fusion.10
  694.0 4.8 fusion.11
  700.5 4.8 fusion.12
  707.0 4.8 fusion.13
  713.5 4.8 fusion.14
  723.9 40.4 %multiply_convert_fusion = bf16[16,10,2,256,256]{4,3,2,1,0:T(8,128)(2,1)} fusion(f32[16,10,2,256,256]{4,3,2,1,0:T(8,128)} %fusion.15), kind=kLoop, calls=%fused_computation | loop fusion | flops 41943040 | bytes 125829120 | tf_op jit(solution)/shard_map/convert_element_type | solution.py:90
  (52 shorter events, 22.2 us)
Async XLA Ops:
  11.1 86.5 %copy-start.21 = (f32[64]{0:T(128)S(1)}, f32[64]{0:T(128)}, u32[]{:S(2)}) copy-start(f32[64]{0:T(128)} %param.10) | copy-start | bytes 772
  308.9 17.4 %copy-start.18 = (s32[10]{0:T(128)S(1)}, s32[10]{0:T(128)}, u32[]{:S(2)}) copy-start(s32[10]{0:T(128)} %param.13) | copy-start | bytes 124
  308.9 18.1 %copy-start.19 = (s32[10]{0:T(128)S(1)}, s32[10]{0:T(128)}, u32[]{:S(2)}) copy-start(s32[10]{0:T(128)} %constant.38.clone) | copy-start | bytes 124
  308.9 18.1 %copy-start.20 = (s32[10]{0:T(128)S(1)}, s32[10]{0:T(128)}, u32[]{:S(2)}) copy-start(s32[10]{0:T(128)} %constant.37.clone) | copy-start | bytes 124
  308.9 199.6 %all-to-all-start = ((bf16[256,2,128,64]{2,3,1,0:T(8,128)(2,1)}), bf16[256,2,128,64]{2,3,1,0:T(8,128)(2,1)}, u32[]{:S(2)}, u32[]{:S(2)}) async-start(bf16[256,2,128,64]{2,3,1,0:T(8,128)(2,1)} %bitcast.110), calls=%async_computation | async-start | bytes 16777216 | tf_op jit(solution)/shard_map/all_to_all | solution.py:88
  661.4 6.6 copy-start.13
  661.4 6.6 copy-start.17
  668.0 4.8 copy-start.11
  668.0 6.5 copy-start.16
  674.5 4.8 copy-start.9
  674.5 6.5 copy-start.15
  681.0 4.8 copy-start.7
  681.0 6.5 copy-start.14
  687.5 4.8 copy-start.5
  687.5 6.5 copy-start.12
  694.0 4.8 copy-start.3
  694.0 6.5 copy-start.10
  700.5 4.8 copy-start.2
  700.5 6.5 copy-start.8
  707.0 4.8 copy-start.1
  707.0 6.5 copy-start.6
  713.5 4.8 copy-start
  713.5 6.5 copy-start.4
where the time goes:
time: 773 us; the launch traced here: 765 us
  other arithmetic  248 us (32%)
  local copies, waits for them, and re-layouts  218 us (28%)
  waiting for transfers between devices  162 us (21%)
  matrix products  84.8 us (11%)
  blocking collectives  21.8 us (3%)
  starting transfers between devices  17.4 us (2%)
  between operations  13.1 us (2%)
    all_to_all x1, waiting for transfers between devices, body(): lax.all_to_all(arranged, 'wide', split_axis=0, concat_axis=3, tiled=True)  162 us
    convert_element_type x1, other arithmetic, body(): filtered = (filtered * input_gain[:, None, None]).astype(jnp.bfloat16)  120 us
    slice x1, local copies, waits for them, and re-layouts, body(): voltages[:, tap_index:tap_index + frames, :].astype(jnp.float32)  86.5 us
    another operation x4, local copies, waits for them, and re-layouts, visibility_terms(): tile_list.append(jnp.stack([real_tile, imag_tile], axis=1))  60.9 us
    unnamed x9, other arithmetic  45.1 us
    convert_element_type x1, other arithmetic, body(): return (summed * jnp.float32(1.0 / frames)).astype(jnp.bfloat16)  40.4 us
    dot_general x1, matrix products, visibility_terms(): jnp.einsum('cfi,cfj->cij', rotated, stacked, preferred_element_type=jnp.f...  29.5 us
    dot_general x1, matrix products, visibility_terms(): jnp.einsum('cfi,cfj->cij', stacked, stacked, preferred_element_type=jnp.f...  29.5 us
  transfers between devices with their start and end apart: 1, of which 1 were waited for; matrix products, arithmetic and copies ran while one was open for 1% of the time, Pallas kernels for 0%

commit v1 on v0

--- a/solution.py
+++ b/solution.py
@@ -1,9 +1,12 @@
+import functools
 import math
 
 import jax
 import jax.numpy as jnp
 import numpy as np
 from jax import lax
+from jax.experimental import pallas as pl
+from jax.experimental.pallas import tpu as pltpu
 from jax.sharding import PartitionSpec as P
 
 BLK = 256
@@ -61,7 +64,7 @@
     return jnp.stack(tile_list, axis=1)
 
 
-def body(voltages, filter_taps, input_gain, input_flags, kept_channels, tile_order):
+def plain_body(voltages, filter_taps, input_gain, input_flags, kept_channels, tile_order):
     local_inputs, padded_frames, samples = voltages.shape
     tap_count = filter_taps.shape[0]
     frames = padded_frames - tap_count + 1
@@ -88,6 +91,245 @@
     turned = lax.all_to_all(arranged, "wide", split_axis=0, concat_axis=3, tiled=True)
     summed = visibility_terms(turned, tile_order, BLK)
     return (summed * jnp.float32(1.0 / frames)).astype(jnp.bfloat16)
+
+
+LANES = 128
+CHUNK = 16
+PIECES = 4
+GROUPS = 2
+PRESCALE = 1024.0
+
+
+def dft_rows(kept_channels, samples):
+    fine = LANES
+    step = jnp.float32(2.0 * math.pi / samples)
+    high = jnp.arange(samples // fine, dtype=jnp.int32) * fine
+    low = jnp.arange(fine, dtype=jnp.int32)
+    angle_h = (kept_channels[:, None] * high[None, :] % samples).astype(jnp.float32) * step
+    angle_l = (kept_channels[:, None] * low[None, :] % samples).astype(jnp.float32) * step
+    factor = jnp.float32(1.0 / math.sqrt(samples / 2))
+    cos_h, sin_h = jnp.cos(angle_h) * factor, jnp.sin(angle_h) * factor
+    cos_l, sin_l = jnp.cos(angle_l), jnp.sin(angle_l)
+    rows = []
+    for step_index in range(samples // fine):
+        ch = cos_h[:, step_index : step_index + 1]
+        sh = sin_h[:, step_index : step_index + 1]
+        rows.append((ch * cos_l - sh * sin_l, -(sh * cos_l + ch * sin_l)))
+    real = jnp.concatenate([r for r, _ in rows], axis=1)
+    imag = jnp.concatenate([m for _, m in rows], axis=1)
+    return jnp.stack([real, imag], axis=1).reshape(-1, samples).astype(jnp.bfloat16)
+
+
+def filter_kernel(main, h0, h1, h2, taps, gain, weight, table, *rest):
+    groups = len(rest) - 2
+    outs, filt, turn = rest[:groups], rest[groups], rest[groups + 1]
+    sub = pl.program_id(0)
+    inputs = main.shape[1]
+    halos = (h0, h1, h2)
+
+    @pl.loop(0, main.shape[2] // LANES)
+    def _(strip):
+        cols = pl.ds(pl.multiple_of(strip * LANES, LANES), LANES)
+        tap_rows = [jnp.broadcast_to(taps[t : t + 1, cols], (16, LANES)) for t in range(4)]
+        for a in range(0, inputs, 16):
+            g = gain[a : a + 16, :]
+            window = [main[f, a : a + 16, cols].astype(jnp.float32) for f in range(3)]
+            for f in range(CHUNK):
+                if f + 3 < CHUNK:
+                    newest = main[f + 3, a : a + 16, cols]
+                else:
+                    newest = halos[f + 3 - CHUNK][0, a : a + 16, cols]
+                window.append(newest.astype(jnp.float32))
+                total = window[0] * tap_rows[0]
+                for t in range(1, 4):
+                    total = total + window[t] * tap_rows[t]
+                filt[f * inputs + a : f * inputs + a + 16, cols] = (total * g).astype(jnp.bfloat16)
+                window = window[1:]
+
+    spectra = lax.dot_general(
+        table[...], filt[...], (((1,), (1,)), ((), ())), preferred_element_type=jnp.float32
+    )
+    lane_rows = CHUNK * inputs // LANES
+    height = 2 * lane_rows
+    w = weight[...]
+    channels = table.shape[0]
+    for j in range(2):
+        @pl.when(sub == j)
+        def _():
+            for r in range(lane_rows):
+                turn[pl.ds(j * lane_rows + r, channels, stride=height), :] = (
+                    spectra[:, r * LANES : (r + 1) * LANES] * w
+                )
+
+    @pl.when(sub == 1)
+    def _():
+        dests, local, _, _, _ = outs[0].shape
+        every = local * groups
+
+        @pl.loop(0, dests)
+        def _(d):
+            for g in range(groups):
+                start = (d * every + g * local) * 2 * height
+                block = turn[pl.ds(pl.multiple_of(start, 2 * height), local * 2 * height), :]
+                outs[g][d] = block.astype(jnp.bfloat16).reshape(local, 2, height, LANES)
+
+
+def filter_piece(piece, turned, taps, gain, weight, table, dests):
+    _, inputs, samples = turned.shape
+    channels = table.shape[0]
+    local = channels // 2 // dests // GROUPS
+    height = 2 * CHUNK * inputs // LANES
+    shape = jax.ShapeDtypeStruct((dests, local, 2, height, LANES), jnp.bfloat16)
+    halo = [
+        pl.BlockSpec((1, inputs, samples), lambda i, j=j: ((piece * 2 + i + 1) * CHUNK + j, 0, 0))
+        for j in range(3)
+    ]
+    whole = lambda x: pl.BlockSpec(x.shape, lambda i: (0, 0))
+    return pl.pallas_call(
+        filter_kernel,
+        grid=(2,),
+        in_specs=[pl.BlockSpec((CHUNK, inputs, samples), lambda i: (piece * 2 + i, 0, 0))]
+        + halo
+        + [whole(taps), whole(gain), whole(weight), whole(table)],
+        out_specs=[pl.BlockSpec(shape.shape, lambda i: (0, 0, 0, 0, 0))] * GROUPS,
+        out_shape=[shape] * GROUPS,
+        scratch_shapes=[
+            pltpu.VMEM((CHUNK * inputs, samples), jnp.bfloat16),
+            pltpu.VMEM((channels * height, LANES), jnp.float32),
+        ],
+        compiler_params=pltpu.CompilerParams(vmem_limit_bytes=52 * 2**20),
+        cost_estimate=pl.CostEstimate(
+            flops=2 * 2 * CHUNK * inputs * samples * channels,
+            bytes_accessed=2 * (CHUNK + 3) * inputs * samples * 2 + 6 * 2**20,
+            transcendentals=0,
+        ),
+        name="filterbank",
+    )(turned, turned, turned, turned, taps, gain, weight, table)
+
+
+def correlate_kernel(slots, *rest, block, frames):
+    pieces = rest[: PIECES]
+    out, stacked, rotated, flipped = rest[PIECES:]
+    sources, _, _, height, _ = pieces[0].shape
+    half = LANES // 2
+    for p in range(PIECES):
+        for part in range(2):
+            for s in range(0, sources, 2):
+                first = pieces[p][s, 0, part]
+                second = pieces[p][s + 1, 0, part]
+                row = part * frames + p * 2 * height
+                cols = slice(s * half, s * half + LANES)
+                stacked[row : row + height, cols] = jnp.concatenate(
+                    [first[:, :half], second[:, :half]], axis=1
+                )
+                stacked[row + height : row + 2 * height, cols] = jnp.concatenate(
+                    [first[:, half:], second[:, half:]], axis=1
+                )
+    inputs = stacked.shape[1]
+    x = stacked[...].astype(jnp.float32)
+    total = jnp.sum(x * x, keepdims=True)
+    power = total / jnp.float32(inputs * frames * PRESCALE * PRESCALE) + jnp.float32(eps_power)
+    scale = lax.rsqrt(power)
+    scale = scale * scale * jnp.float32(1.0 / (frames * PRESCALE * PRESCALE))
+    flipped[...] = stacked[...].T
+    rotated[:frames, :] = -stacked[frames:, :]
+    rotated[frames:, :] = stacked[:frames, :]
+    blocks = inputs // block
+    row_table, col_table = tile_tables(blocks)
+    for c in range(blocks):
+        cols = slice(c * block, (c + 1) * block)
+        for r in range(c + 1):
+            tile = [t for t in range(len(row_table)) if row_table[t] == r and col_table[t] == c][0]
+            slot = slots[tile]
+            left = flipped[r * block : (r + 1) * block, :]
+            for part, right in ((0, stacked), (1, rotated)):
+                gram = jnp.dot(left, right[:, cols], preferred_element_type=jnp.float32)
+                out[0, slot, part] = (gram * scale).astype(jnp.bfloat16)
+
+
+def correlate(slots, pieces, offset, total, previous):
+    sources, local, _, height, _ = pieces[0].shape
+    inputs = sources * LANES // 2
+    frames = PIECES * height * 2
+    tiles = slots.shape[0]
+    in_specs = [pl.BlockSpec((sources, 1, 2, height, LANES), lambda k, *_: (0, k, 0, 0, 0))] * PIECES
+    operands = [slots, *pieces]
+    kernel = functools.partial(correlate_kernel, block=BLK, frames=frames)
+    aliases = {}
+    if previous is not None:
+        base = kernel
+        kernel = lambda s, prev, *rest: base(s, *rest)
+        in_specs = [pl.BlockSpec(memory_space=pl.ANY)] + in_specs
+        operands = [slots, previous, *pieces]
+        aliases = {1: 0}
+    return pl.pallas_call(
+        kernel,
+        grid_spec=pltpu.PrefetchScalarGridSpec(
+            num_scalar_prefetch=1,
+            grid=(local,),
+            in_specs=in_specs,
+            out_specs=pl.BlockSpec(
+                (1, tiles, 2, BLK, BLK), lambda k, *_: (k + offset, 0, 0, 0, 0)
+            ),
+            scratch_shapes=[
+                pltpu.VMEM((2 * frames, inputs), jnp.bfloat16),
+                pltpu.VMEM((2 * frames, inputs), jnp.bfloat16),
+                pltpu.VMEM((inputs, 2 * frames), jnp.bfloat16),
+            ],
+        ),
+        out_shape=jax.ShapeDtypeStruct((total, tiles, 2, BLK, BLK), jnp.bfloat16),
+        input_output_aliases=aliases,
+        compiler_params=pltpu.CompilerParams(vmem_limit_bytes=40 * 2**20),
+        cost_estimate=pl.CostEstimate(
+            flops=local * tiles * 2 * 2 * BLK * BLK * 2 * frames,
+            bytes_accessed=local * (tiles * 2 * BLK * BLK * 2 + inputs * frames * 4),
+            transcendentals=0,
+        ),
+        name="correlate",
+    )(*operands)
+
+
+def body(voltages, filter_taps, input_gain, input_flags, kept_channels, tile_order):
+    local_inputs, padded_frames, samples = voltages.shape
+    taps = filter_taps.shape[0]
+    frames = padded_frames - taps + 1
+    kept = kept_channels.shape[0]
+    devices = lax.axis_size("wide")
+    fits = (
+        local_inputs * 2 == LANES
+        and taps == 4
+        and frames == PIECES * 2 * CHUNK
+        and devices % 2 == 0
+        and kept % (devices * GROUPS) == 0
+        and samples % LANES == 0
+    )
+    if not fits:
+        return plain_body(
+            voltages, filter_taps, input_gain, input_flags, kept_channels, tile_order
+        )
+    table = dft_rows(kept_channels, samples)
+    turned = jnp.transpose(voltages, (1, 0, 2))
+    gain = jnp.broadcast_to(input_gain[:, None], (local_inputs, LANES))
+    weight = input_flags.astype(jnp.float32) * jnp.float32(PRESCALE)
+    weight = jnp.concatenate([weight, weight])[None, :]
+    float_taps = filter_taps.astype(jnp.float32)
+    tiles = tile_order.shape[0]
+    numbers = jnp.arange(tiles, dtype=jnp.int32)
+    slots = jnp.sum(
+        jnp.where(tile_order[None, :] == numbers[:, None], numbers[None, :], 0), axis=1
+    ).astype(jnp.int32)
+    received = [[] for _ in range(GROUPS)]
+    for piece in range(PIECES):
+        outs = filter_piece(piece, turned, float_taps, gain, weight, table, devices)
+        for g in range(GROUPS):
+            received[g].append(
+                lax.all_to_all(outs[g], "wide", split_axis=0, concat_axis=0, tiled=True)
+            )
+    local = kept // devices
+    result = None
+    for g in range(GROUPS):
+        result = correlate(slots, received[g], g * (local // GROUPS), local, result)
+    return result
 
 
 def solution(mesh):

time: 773 us -> 301 us (0.39)
  other arithmetic: 248 us -> 23.1 us
  local copies, waits for them, and re-layouts: 218 us -> 10.5 us
  waiting for transfers between devices: 162 us -> 27.5 us
  blocking collectives: 21.8 us -> 121 us
  Pallas kernels: 0 us -> 98.4 us
  matrix products: 84.8 us -> 0 us
  between operations: 13.1 us -> 0.11 us
    convert_element_type x5 -> x1, other arithmetic: 171 us -> 0.73 us  [body(): float_taps = filter_taps.astype(jnp.float32)]
    all_to_all x1 -> x4, waiting for transfers between devices: 162 us -> 27.5 us  [body(): lax.all_to_all(outs[g], 'wide', split_axis=0, concat_axis=0, tiled=True)]
    all_to_all x0 -> x4, blocking collectives: none -> 121 us  [body(): lax.all_to_all(outs[g], 'wide', split_axis=0, concat_axis=0, tiled=True)]
    pallas_call x0 -> x6, Pallas kernels: none -> 98.4 us  [the longest x4 68.9 us: filter_piece(): pl.pallas_call(filter_kernel, grid=(2,), in_specs=[pl.BlockSpec((CHUNK, i...]
    slice x3 -> x2, local copies, waits for them, and re-layouts: 93 us -> 0.03 us  [the longest x1 0.02 us: dft_rows(): ch = cos_h[:, step_index:step_index + 1]]
    dot_general x3 -> x0, matrix products: 84.8 us -> none  [the longest x1 29.5 us: visibility_terms(): jnp.einsum('cfi,cfj->cij', rotated, stacked, preferred_element_type=jnp.f...]
    another operation x4 -> x1, local copies, waits for them, and re-layouts: 60.9 us -> 2.34 us  [dft_rows(): jnp.stack([real, imag], axis=1).reshape(-1, samples).astype(jnp.bfloat16)]
    reshape x2 -> x0, local copies, waits for them, and re-layouts: 27.9 us -> none  [body(): equalized.reshape(local_inputs, frames, 2, kept).transpose(3, 2, 1, 0)]
  transfers between devices with their start and end apart: 1 -> 4, of which waited for: 1 -> 4; matrix products, arithmetic and copies ran while one was open for 1% -> 0% of each run, Pallas kernels for 0% -> 22%
where the time goes in v1:
time: 301 us; the launch traced here: 300 us
  blocking collectives  121 us (40%)
  Pallas kernels  98.4 us (33%)
  waiting for transfers between devices  27.5 us (9%)
  other arithmetic  23.1 us (8%)
  starting transfers between devices  20 us (7%)
  local copies, waits for them, and re-layouts  10.5 us (3%)
    all_to_all x4, blocking collectives, body(): lax.all_to_all(outs[g], 'wide', split_axis=0, concat_axis=0, tiled=True)  121 us
    pallas_call x4, Pallas kernels, filter_piece(): pl.pallas_call(filter_kernel, grid=(2,), in_specs=[pl.BlockSpec((CHUNK, i...  68.9 us
    pallas_call x2, Pallas kernels, correlate(): pl.pallas_call(kernel, grid_spec=pltpu.PrefetchScalarGridSpec(num_scalar_...  29.6 us
    all_to_all x4, waiting for transfers between devices, body(): lax.all_to_all(outs[g], 'wide', split_axis=0, concat_axis=0, tiled=True)  27.5 us
    all_to_all x4, starting transfers between devices, body(): lax.all_to_all(outs[g], 'wide', split_axis=0, concat_axis=0, tiled=True)  20 us
    unnamed x15, other arithmetic  19.8 us
  transfers between devices with their start and end apart: 4, of which 4 were waited for; matrix products, arithmetic and copies ran while one was open for 0% of the time, Pallas kernels for 22%

profile of v1, /device:TPU:15, one launch (start us, length us, event | category | flops | bytes accessed | tf_op | source)
XLA Modules:
  0.0 300.3 jit_solution(3094678265493575022)
XLA Ops:
  3.7 1.4 constant_dynamic-update-slice_fusion.14
  5.1 1.4 constant_dynamic-update-slice_fusion.13
  6.4 1.4 constant_dynamic-update-slice_fusion.12
  7.8 1.4 constant_dynamic-update-slice_fusion.11
  9.2 1.4 constant_dynamic-update-slice_fusion.10
  10.5 1.4 constant_dynamic-update-slice_fusion.9
  11.9 1.4 constant_dynamic-update-slice_fusion.8
  13.3 1.4 constant_dynamic-update-slice_fusion.7
  14.7 1.4 constant_dynamic-update-slice_fusion.6
  16.0 1.4 constant_dynamic-update-slice_fusion.5
  17.4 1.4 constant_dynamic-update-slice_fusion.4
  18.8 1.4 constant_dynamic-update-slice_fusion.3
  23.1 2.3 copy.10
  25.5 2.2 convert_element_type.19.table
  27.8 17.2 %filterbank.7 = (bf16[16,8,2,16,128]{4,3,2,1,0:T(8,128)(2,1)S(1)}, bf16[16,8,2,16,128]{4,3,2,1,0:T(8,128)(2,1)}) custom-call(bf16[131,64,2048]{2,1,0:T(8,128)(2,1)} %bitcast.37, bf16[131,64,2048]{2,1,0:T(8,128)(2,1)} %bitcast.38, bf16[131,64,2048]{2,1,0:T(8,128)(2,1)} %bitcast.39, bf16[131,64,2048]{2,1,0:T(8,128)(2,1)} %bitcast.40, ...), custom_call_target="tpu_custom_call" | custom-call | flops 4294967296 | bytes 16252928 | tf_op jit(solution)/shard_map/filterbank/pallas_call | solution.py:188
  44.9 31.3 %all_to_all.40.rest_3_ = bf16[16,8,2,16,128]{4,3,2,1,0:T(8,128)(2,1)} all-to-all(bf16[16,8,2,16,128]{4,3,2,1,0:T(8,128)(2,1)S(1)} %get-tuple-element.16), channel_id=1, replica_groups=mesh['grp'=2,'wide'=16] {'wide'}, dimensions={0} | all-to-all | bytes 2097152 | tf_op jit(solution)/shard_map/all_to_all | solution.py:326
  76.2 5.0 %all-to-all-start.7 = ((bf16[16,8,2,16,128]{4,3,2,1,0:T(8,128)(2,1)}), bf16[16,8,2,16,128]{4,3,2,1,0:T(8,128)(2,1)S(1)}, u32[]{:S(2)}, u32[]{:S(2)}) async-start(bf16[16,8,2,16,128]{4,3,2,1,0:T(8,128)(2,1)} %get-tuple-element.20), calls=%async_computation.7 | async-start | bytes 2097152 | tf_op jit(solution)/shard_map/all_to_all | solution.py:326
  81.2 17.2 %filterbank.6 = (bf16[16,8,2,16,128]{4,3,2,1,0:T(8,128)(2,1)S(1)}, bf16[16,8,2,16,128]{4,3,2,1,0:T(8,128)(2,1)}) custom-call(bf16[131,64,2048]{2,1,0:T(8,128)(2,1)} %bitcast.41, bf16[131,64,2048]{2,1,0:T(8,128)(2,1)} %bitcast.42, bf16[131,64,2048]{2,1,0:T(8,128)(2,1)} %bitcast.43, bf16[131,64,2048]{2,1,0:T(8,128)(2,1)} %bitcast.44, ...), custom_call_target="tpu_custom_call" | custom-call | flops 4294967296 | bytes 16252928 | tf_op jit(solution)/shard_map/filterbank/pallas_call | solution.py:188
  98.4 7.7 %all-to-all-done.7.rest_3_ = bf16[16,8,2,16,128]{4,3,2,1,0:T(8,128)(2,1)S(1)} async-done(((bf16[16,8,2,16,128]{4,3,2,1,0:T(8,128)(2,1)}), bf16[16,8,2,16,128]{4,3,2,1,0:T(8,128)(2,1)S(1)}, u32[]{:S(2)}, u32[]{:S(2)}) %all-to-all-start.7) | async-done | bytes 1048608 | tf_op jit(solution)/shard_map/all_to_all | solution.py:326
  106.1 29.7 %all_to_all.41.rest_2_ = bf16[16,8,2,16,128]{4,3,2,1,0:T(8,128)(2,1)} all-to-all(bf16[16,8,2,16,128]{4,3,2,1,0:T(8,128)(2,1)S(1)} %get-tuple-element.15), channel_id=1, replica_groups=mesh['grp'=2,'wide'=16] {'wide'}, dimensions={0} | all-to-all | bytes 2097152 | tf_op jit(solution)/shard_map/all_to_all | solution.py:326
  135.8 5.0 %all-to-all-start.6 = ((bf16[16,8,2,16,128]{4,3,2,1,0:T(8,128)(2,1)}), bf16[16,8,2,16,128]{4,3,2,1,0:T(8,128)(2,1)S(1)}, u32[]{:S(2)}, u32[]{:S(2)}) async-start(bf16[16,8,2,16,128]{4,3,2,1,0:T(8,128)(2,1)} %get-tuple-element.19), calls=%async_computation.6 | async-start | bytes 2097152 | tf_op jit(solution)/shard_map/all_to_all | solution.py:326
  140.8 17.3 %filterbank.5 = (bf16[16,8,2,16,128]{4,3,2,1,0:T(8,128)(2,1)S(1)}, bf16[16,8,2,16,128]{4,3,2,1,0:T(8,128)(2,1)}) custom-call(bf16[131,64,2048]{2,1,0:T(8,128)(2,1)} %bitcast.45, bf16[131,64,2048]{2,1,0:T(8,128)(2,1)} %bitcast.46, bf16[131,64,2048]{2,1,0:T(8,128)(2,1)} %bitcast.47, bf16[131,64,2048]{2,1,0:T(8,128)(2,1)} %bitcast.48, ...), custom_call_target="tpu_custom_call" | custom-call | flops 4294967296 | bytes 16252928 | tf_op jit(solution)/shard_map/filterbank/pallas_call | solution.py:188
  158.1 7.6 %all-to-all-done.6.rest_2_ = bf16[16,8,2,16,128]{4,3,2,1,0:T(8,128)(2,1)S(1)} async-done(((bf16[16,8,2,16,128]{4,3,2,1,0:T(8,128)(2,1)}), bf16[16,8,2,16,128]{4,3,2,1,0:T(8,128)(2,1)S(1)}, u32[]{:S(2)}, u32[]{:S(2)}) %all-to-all-start.6) | async-done | bytes 1048608 | tf_op jit(solution)/shard_map/all_to_all | solution.py:326
  165.7 29.7 %all_to_all.42.rest_1_ = bf16[16,8,2,16,128]{4,3,2,1,0:T(8,128)(2,1)} all-to-all(bf16[16,8,2,16,128]{4,3,2,1,0:T(8,128)(2,1)S(1)} %get-tuple-element.14), channel_id=1, replica_groups=mesh['grp'=2,'wide'=16] {'wide'}, dimensions={0} | all-to-all | bytes 2097152 | tf_op jit(solution)/shard_map/all_to_all | solution.py:326
  195.3 5.0 %all-to-all-start.5 = ((bf16[16,8,2,16,128]{4,3,2,1,0:T(8,128)(2,1)}), bf16[16,8,2,16,128]{4,3,2,1,0:T(8,128)(2,1)S(1)}, u32[]{:S(2)}, u32[]{:S(2)}) async-start(bf16[16,8,2,16,128]{4,3,2,1,0:T(8,128)(2,1)} %get-tuple-element.18), calls=%async_computation.5 | async-start | bytes 2097152 | tf_op jit(solution)/shard_map/all_to_all | solution.py:326
  200.3 17.2 %filterbank.4 = (bf16[16,8,2,16,128]{4,3,2,1,0:T(8,128)(2,1)S(1)}, bf16[16,8,2,16,128]{4,3,2,1,0:T(8,128)(2,1)}) custom-call(bf16[131,64,2048]{2,1,0:T(8,128)(2,1)} %bitcast.49, bf16[131,64,2048]{2,1,0:T(8,128)(2,1)} %bitcast.50, bf16[131,64,2048]{2,1,0:T(8,128)(2,1)} %bitcast.51, bf16[131,64,2048]{2,1,0:T(8,128)(2,1)} %bitcast.52, ...), custom_call_target="tpu_custom_call" | custom-call | flops 4294967296 | bytes 16252928 | tf_op jit(solution)/shard_map/filterbank/pallas_call | solution.py:188
  218.5 6.7 %all-to-all-done.5.rest_1_ = bf16[16,8,2,16,128]{4,3,2,1,0:T(8,128)(2,1)S(1)} async-done(((bf16[16,8,2,16,128]{4,3,2,1,0:T(8,128)(2,1)}), bf16[16,8,2,16,128]{4,3,2,1,0:T(8,128)(2,1)S(1)}, u32[]{:S(2)}, u32[]{:S(2)}) %all-to-all-start.5) | async-done | bytes 1048608 | tf_op jit(solution)/shard_map/all_to_all | solution.py:326
  225.2 30.0 %all_to_all.43.rest_0_ = bf16[16,8,2,16,128]{4,3,2,1,0:T(8,128)(2,1)} all-to-all(bf16[16,8,2,16,128]{4,3,2,1,0:T(8,128)(2,1)} %copy-done.4), channel_id=1, replica_groups=mesh['grp'=2,'wide'=16] {'wide'}, dimensions={0} | all-to-all | bytes 2097152 | tf_op jit(solution)/shard_map/all_to_all | solution.py:326
  255.2 5.0 %all-to-all-start.4 = ((bf16[16,8,2,16,128]{4,3,2,1,0:T(8,128)(2,1)}), bf16[16,8,2,16,128]{4,3,2,1,0:T(8,128)(2,1)}, u32[]{:S(2)}, u32[]{:S(2)}) async-start(bf16[16,8,2,16,128]{4,3,2,1,0:T(8,128)(2,1)} %get-tuple-element.17), calls=%async_computation.4 | async-start | bytes 2097152 | tf_op jit(solution)/shard_map/all_to_all | solution.py:326
  265.2 14.4 %correlate.2.prev = bf16[16,10,2,256,256]{4,3,2,1,0:T(8,128)(2,1)} custom-call(s32[10]{0:T(128)S(1)} %select_reduce_fusion.slots.s, bf16[16,8,2,16,128]{4,3,2,1,0:T(8,128)(2,1)S(1)} %copy-done.3, bf16[16,8,2,16,128]{4,3,2,1,0:T(8,128)(2,1)S(1)} %copy-done.2, bf16[16,8,2,16,128]{4,3,2,1,0:T(8,128)(2,1)S(1)} %copy-done.1, bf16[16,8,2,16,128]{4,3,2,1,0:T(8,128)(2,1)S(1)} %copy-done), custom_call_target="tpu_custom_call" | custom-call | flops 5368709120 | bytes 25165824 | tf_op jit(solution)/shard_map/correlate/pallas_call | solution.py:265
  279.7 5.5 %all-to-all-done.4.rest_0_ = bf16[16,8,2,16,128]{4,3,2,1,0:T(8,128)(2,1)} async-done(((bf16[16,8,2,16,128]{4,3,2,1,0:T(8,128)(2,1)}), bf16[16,8,2,16,128]{4,3,2,1,0:T(8,128)(2,1)}, u32[]{:S(2)}, u32[]{:S(2)}) %all-to-all-start.4) | async-done | bytes 1048608 | tf_op jit(solution)/shard_map/all_to_all | solution.py:326
  285.2 15.1 %correlate.3 = bf16[16,10,2,256,256]{4,3,2,1,0:T(8,128)(2,1)} custom-call(s32[10]{0:T(128)S(1)} %select_reduce_fusion.slots.s, bf16[16,10,2,256,256]{4,3,2,1,0:T(8,128)(2,1)} %correlate.2.prev, bf16[16,8,2,16,128]{4,3,2,1,0:T(8,128)(2,1)} %all-to-all-done.4.rest_0_, ...), custom_call_target="tpu_custom_call", output_to_operand_aliasing={{}: (1, {})} | custom-call | flops 5368709120 | bytes 25165824 | tf_op jit(solution)/shard_map/correlate/pallas_call | solution.py:265
  (30 shorter events, 12.7 us)
Async XLA Ops:
  0.0 21.5 %copy-start.5 = (s32[256]{0:T(256)S(1)}, s32[256]{0:T(256)}, u32[]{:S(2)}) copy-start(s32[256]{0:T(256)} %param.10) | copy-start | bytes 3076
  25.5 2.2 copy-start.6
  76.2 29.9 %all-to-all-start.7 = ((bf16[16,8,2,16,128]{4,3,2,1,0:T(8,128)(2,1)}), bf16[16,8,2,16,128]{4,3,2,1,0:T(8,128)(2,1)S(1)}, u32[]{:S(2)}, u32[]{:S(2)}) async-start(bf16[16,8,2,16,128]{4,3,2,1,0:T(8,128)(2,1)} %get-tuple-element.20), calls=%async_computation.7 | async-start | bytes 2097152 | tf_op jit(solution)/shard_map/all_to_all | solution.py:326
  135.8 29.9 %all-to-all-start.6 = ((bf16[16,8,2,16,128]{4,3,2,1,0:T(8,128)(2,1)}), bf16[16,8,2,16,128]{4,3,2,1,0:T(8,128)(2,1)S(1)}, u32[]{:S(2)}, u32[]{:S(2)}) async-start(bf16[16,8,2,16,128]{4,3,2,1,0:T(8,128)(2,1)} %get-tuple-element.19), calls=%async_computation.6 | async-start | bytes 2097152 | tf_op jit(solution)/shard_map/all_to_all | solution.py:326
  195.3 29.9 %all-to-all-start.5 = ((bf16[16,8,2,16,128]{4,3,2,1,0:T(8,128)(2,1)}), bf16[16,8,2,16,128]{4,3,2,1,0:T(8,128)(2,1)S(1)}, u32[]{:S(2)}, u32[]{:S(2)}) async-start(bf16[16,8,2,16,128]{4,3,2,1,0:T(8,128)(2,1)} %get-tuple-element.18), calls=%async_computation.5 | async-start | bytes 2097152 | tf_op jit(solution)/shard_map/all_to_all | solution.py:326
  217.5 1.0 copy-start.4
  225.2 35.0 %copy-start.7 = (s32[10]{0:T(128)S(1)}, s32[10]{0:T(128)}, u32[]{:S(2)}) copy-start(s32[10]{0:T(128)} %param.11) | copy-start | bytes 124
  255.2 30.0 %all-to-all-start.4 = ((bf16[16,8,2,16,128]{4,3,2,1,0:T(8,128)(2,1)}), bf16[16,8,2,16,128]{4,3,2,1,0:T(8,128)(2,1)}, u32[]{:S(2)}, u32[]{:S(2)}) async-start(bf16[16,8,2,16,128]{4,3,2,1,0:T(8,128)(2,1)} %get-tuple-element.17), calls=%async_computation.4 | async-start | bytes 2097152 | tf_op jit(solution)/shard_map/all_to_all | solution.py:326
  260.3 1.2 copy-start
  261.6 1.2 copy-start.1
  262.8 1.2 copy-start.2
  264.0 1.2 copy-start.3

commit v2 on v1

--- a/solution.py
+++ b/solution.py
@@ -96,7 +96,7 @@
 LANES = 128
 CHUNK = 16
 PIECES = 4
-GROUPS = 2
+GROUPS = 1
 PRESCALE = 1024.0
 
 
@@ -110,6 +110,7 @@
     factor = jnp.float32(1.0 / math.sqrt(samples / 2))
     cos_h, sin_h = jnp.cos(angle_h) * factor, jnp.sin(angle_h) * factor
     cos_l, sin_l = jnp.cos(angle_l), jnp.sin(angle_l)
+    cos_h, sin_h, cos_l, sin_l = lax.optimization_barrier((cos_h, sin_h, cos_l, sin_l))
     rows = []
     for step_index in range(samples // fine):
         ch = cos_h[:, step_index : step_index + 1]

time: 301 us -> 268 us (0.89)
  blocking collectives: 121 us -> 0 us
  waiting for transfers between devices: 27.5 us -> 137 us
  other arithmetic: 23.1 us -> 6.5 us
  local copies, waits for them, and re-layouts: 10.5 us -> 4.48 us
    all_to_all x4 -> x0, blocking collectives: 121 us -> none  [body(): lax.all_to_all(outs[g], 'wide', split_axis=0, concat_axis=0, tiled=True)]
    all_to_all x4, waiting for transfers between devices: 27.5 us -> 137 us  [body(): lax.all_to_all(outs[g], 'wide', split_axis=0, concat_axis=0, tiled=True)]
    unnamed x15, other arithmetic: 19.8 us -> 2.46 us
    unnamed x16 -> x4, local copies, waits for them, and re-layouts: 5.88 us -> 0.01 us
    pallas_call x2 -> x1, Pallas kernels: 29.6 us -> 27.4 us  [correlate(): pl.pallas_call(kernel, grid_spec=pltpu.PrefetchScalarGridSpec(num_scalar_...]
  transfers between devices with their start and end apart: 4 -> 4, of which waited for: 4 -> 4; matrix products, arithmetic and copies ran while one was open for 0% -> 0% of each run, Pallas kernels for 22% -> 20%
where the time goes in v2:
time: 268 us; the launch traced here: 267 us
  waiting for transfers between devices  137 us (51%)
  Pallas kernels  97.6 us (36%)
  starting transfers between devices  21.3 us (8%)
  other arithmetic  6.5 us (2%)
  local copies, waits for them, and re-layouts  4.48 us (2%)
    all_to_all x4, waiting for transfers between devices, body(): lax.all_to_all(outs[g], 'wide', split_axis=0, concat_axis=0, tiled=True)  137 us
    pallas_call x4, Pallas kernels, filter_piece(): pl.pallas_call(filter_kernel, grid=(2,), in_specs=[pl.BlockSpec((CHUNK, i...  70.2 us
    pallas_call x1, Pallas kernels, correlate(): pl.pallas_call(kernel, grid_spec=pltpu.PrefetchScalarGridSpec(num_scalar_...  27.4 us
    all_to_all x4, starting transfers between devices, body(): lax.all_to_all(outs[g], 'wide', split_axis=0, concat_axis=0, tiled=True)  21.3 us
  transfers between devices with their start and end apart: 4, of which 4 were waited for; matrix products, arithmetic and copies ran while one was open for 0% of the time, Pallas kernels for 20%

profile of v2, /device:TPU:15, one launch (start us, length us, event | category | flops | bytes accessed | tf_op | source)
XLA Modules:
  0.0 267.2 jit_solution(16080179109884230579)
XLA Ops:
  0.0 0.7 convert_multiply_fusion
  0.7 1.3 fusion.6
  2.0 0.8 sine_multiply_fusion
  2.8 0.7 convert_element_type.15.taps
  3.8 0.2 constant_dynamic-update-slice_fusion.14
  3.9 0.2 constant_dynamic-update-slice_fusion.13
  4.3 0.2 constant_dynamic-update-slice_fusion.11
  4.6 0.2 constant_dynamic-update-slice_fusion.9
  4.8 0.2 constant_dynamic-update-slice_fusion.8
  5.0 0.2 constant_dynamic-update-slice_fusion.7
  5.1 0.2 constant_dynamic-update-slice_fusion.6
  5.3 0.2 constant_dynamic-update-slice_fusion.5
  5.5 0.2 constant_dynamic-update-slice_fusion.4
  5.8 0.2 constant_dynamic-update-slice_fusion.2
  6.0 0.2 constant_dynamic-update-slice_fusion.1
  6.2 0.2 constant_dynamic-update-slice_fusion
  6.4 0.2 pad_maximum_fusion
  6.6 2.2 copy.9
  8.7 2.2 convert_element_type.19.table
  11.0 17.5 %filterbank.7 = bf16[16,16,2,16,128]{4,3,2,1,0:T(8,128)(2,1)} custom-call(bf16[131,64,2048]{2,1,0:T(8,128)(2,1)} %bitcast.37, bf16[131,64,2048]{2,1,0:T(8,128)(2,1)} %bitcast.38, bf16[131,64,2048]{2,1,0:T(8,128)(2,1)} %bitcast.39, bf16[131,64,2048]{2,1,0:T(8,128)(2,1)} %bitcast.40, f32[4,2048]{1,0:T(4,128)S(1)} %convert_element_type.15.taps, ...), custom_call_target="tpu_custom_call" | custom-call | flops 4294967296 | bytes 16252928 | tf_op jit(solution)/shard_map/filterbank/pallas_call | solution.py:189
  28.6 6.6 %all-to-all-start.3 = ((bf16[16,16,2,16,128]{4,3,2,1,0:T(8,128)(2,1)}), bf16[16,16,2,16,128]{4,3,2,1,0:T(8,128)(2,1)S(1)}, u32[]{:S(2)}, u32[]{:S(2)}) async-start(bf16[16,16,2,16,128]{4,3,2,1,0:T(8,128)(2,1)} %filterbank.7), calls=%async_computation.3 | async-start | bytes 4194304 | tf_op jit(solution)/shard_map/all_to_all | solution.py:327
  35.1 17.5 %filterbank.6 = bf16[16,16,2,16,128]{4,3,2,1,0:T(8,128)(2,1)} custom-call(bf16[131,64,2048]{2,1,0:T(8,128)(2,1)} %bitcast.41, bf16[131,64,2048]{2,1,0:T(8,128)(2,1)} %bitcast.42, bf16[131,64,2048]{2,1,0:T(8,128)(2,1)} %bitcast.43, bf16[131,64,2048]{2,1,0:T(8,128)(2,1)} %bitcast.44, f32[4,2048]{1,0:T(4,128)S(1)} %convert_element_type.15.taps, ...), custom_call_target="tpu_custom_call" | custom-call | flops 4294967296 | bytes 16252928 | tf_op jit(solution)/shard_map/filterbank/pallas_call | solution.py:189
  52.6 29.9 %all-to-all-done.3.rest_3_ = bf16[16,16,2,16,128]{4,3,2,1,0:T(8,128)(2,1)S(1)} async-done(((bf16[16,16,2,16,128]{4,3,2,1,0:T(8,128)(2,1)}), bf16[16,16,2,16,128]{4,3,2,1,0:T(8,128)(2,1)S(1)}, u32[]{:S(2)}, u32[]{:S(2)}) %all-to-all-start.3) | async-done | bytes 2097184 | tf_op jit(solution)/shard_map/all_to_all | solution.py:327
  82.5 4.9 %all-to-all-start.2 = ((bf16[16,16,2,16,128]{4,3,2,1,0:T(8,128)(2,1)}), bf16[16,16,2,16,128]{4,3,2,1,0:T(8,128)(2,1)}, u32[]{:S(2)}, u32[]{:S(2)}) async-start(bf16[16,16,2,16,128]{4,3,2,1,0:T(8,128)(2,1)} %filterbank.6), calls=%async_computation.2 | async-start | bytes 4194304 | tf_op jit(solution)/shard_map/all_to_all | solution.py:327
  87.4 17.6 %filterbank.4 = bf16[16,16,2,16,128]{4,3,2,1,0:T(8,128)(2,1)} custom-call(bf16[131,64,2048]{2,1,0:T(8,128)(2,1)} %bitcast.45, bf16[131,64,2048]{2,1,0:T(8,128)(2,1)} %bitcast.46, bf16[131,64,2048]{2,1,0:T(8,128)(2,1)} %bitcast.47, bf16[131,64,2048]{2,1,0:T(8,128)(2,1)} %bitcast.48, f32[4,2048]{1,0:T(4,128)S(1)} %convert_element_type.15.taps, ...), custom_call_target="tpu_custom_call" | custom-call | flops 4294967296 | bytes 16252928 | tf_op jit(solution)/shard_map/filterbank/pallas_call | solution.py:189
  105.0 30.0 %all-to-all-done.2.rest_2_ = bf16[16,16,2,16,128]{4,3,2,1,0:T(8,128)(2,1)} async-done(((bf16[16,16,2,16,128]{4,3,2,1,0:T(8,128)(2,1)}), bf16[16,16,2,16,128]{4,3,2,1,0:T(8,128)(2,1)}, u32[]{:S(2)}, u32[]{:S(2)}) %all-to-all-start.2) | async-done | bytes 2097184 | tf_op jit(solution)/shard_map/all_to_all | solution.py:327
  135.0 4.9 %all-to-all-start = ((bf16[16,16,2,16,128]{4,3,2,1,0:T(8,128)(2,1)}), bf16[16,16,2,16,128]{4,3,2,1,0:T(8,128)(2,1)}, u32[]{:S(2)}, u32[]{:S(2)}) async-start(bf16[16,16,2,16,128]{4,3,2,1,0:T(8,128)(2,1)} %filterbank.4), calls=%async_computation | async-start | bytes 4194304 | tf_op jit(solution)/shard_map/all_to_all | solution.py:327
  139.9 17.6 %filterbank.5 = bf16[16,16,2,16,128]{4,3,2,1,0:T(8,128)(2,1)} custom-call(bf16[131,64,2048]{2,1,0:T(8,128)(2,1)} %bitcast.49, bf16[131,64,2048]{2,1,0:T(8,128)(2,1)} %bitcast.50, bf16[131,64,2048]{2,1,0:T(8,128)(2,1)} %bitcast.51, bf16[131,64,2048]{2,1,0:T(8,128)(2,1)} %bitcast.52, f32[4,2048]{1,0:T(4,128)S(1)} %convert_element_type.15.taps, ...), custom_call_target="tpu_custom_call" | custom-call | flops 4294967296 | bytes 16252928 | tf_op jit(solution)/shard_map/filterbank/pallas_call | solution.py:189
  157.5 29.9 %all-to-all-done.rest_0_ = bf16[16,16,2,16,128]{4,3,2,1,0:T(8,128)(2,1)} async-done(((bf16[16,16,2,16,128]{4,3,2,1,0:T(8,128)(2,1)}), bf16[16,16,2,16,128]{4,3,2,1,0:T(8,128)(2,1)}, u32[]{:S(2)}, u32[]{:S(2)}) %all-to-all-start) | async-done | bytes 2097184 | tf_op jit(solution)/shard_map/all_to_all | solution.py:327
  187.4 4.9 %all-to-all-start.1 = ((bf16[16,16,2,16,128]{4,3,2,1,0:T(8,128)(2,1)}), bf16[16,16,2,16,128]{4,3,2,1,0:T(8,128)(2,1)}, u32[]{:S(2)}, u32[]{:S(2)}) async-start(bf16[16,16,2,16,128]{4,3,2,1,0:T(8,128)(2,1)} %filterbank.5), calls=%async_computation.1 | async-start | bytes 4194304 | tf_op jit(solution)/shard_map/all_to_all | solution.py:327
  192.4 47.4 %all-to-all-done.1.rest_1_ = bf16[16,16,2,16,128]{4,3,2,1,0:T(8,128)(2,1)} async-done(((bf16[16,16,2,16,128]{4,3,2,1,0:T(8,128)(2,1)}), bf16[16,16,2,16,128]{4,3,2,1,0:T(8,128)(2,1)}, u32[]{:S(2)}, u32[]{:S(2)}) %all-to-all-start.1) | async-done | bytes 2097184 | tf_op jit(solution)/shard_map/all_to_all | solution.py:327
  239.8 27.4 %correlate.1 = bf16[16,10,2,256,256]{4,3,2,1,0:T(8,128)(2,1)} custom-call(s32[10]{0:T(128)S(1)} %select_reduce_fusion.slots, bf16[16,16,2,16,128]{4,3,2,1,0:T(8,128)(2,1)} %all-to-all-done.rest_0_, bf16[16,16,2,16,128]{4,3,2,1,0:T(8,128)(2,1)} %all-to-all-done.1.rest_1_, bf16[16,16,2,16,128]{4,3,2,1,0:T(8,128)(2,1)} %all-to-all-done.2.rest_2_, ...), custom_call_target="tpu_custom_call" | custom-call | flops 10737418240 | bytes 50331648 | tf_op jit(solution)/shard_map/correlate/pallas_call | solution.py:266
  (14 shorter events, 0.9 us)
Async XLA Ops:
  8.7 2.2 copy-start
  28.6 54.0 %all-to-all-start.3 = ((bf16[16,16,2,16,128]{4,3,2,1,0:T(8,128)(2,1)}), bf16[16,16,2,16,128]{4,3,2,1,0:T(8,128)(2,1)S(1)}, u32[]{:S(2)}, u32[]{:S(2)}) async-start(bf16[16,16,2,16,128]{4,3,2,1,0:T(8,128)(2,1)} %filterbank.7), calls=%async_computation.3 | async-start | bytes 4194304 | tf_op jit(solution)/shard_map/all_to_all | solution.py:327
  82.5 52.4 %all-to-all-start.2 = ((bf16[16,16,2,16,128]{4,3,2,1,0:T(8,128)(2,1)}), bf16[16,16,2,16,128]{4,3,2,1,0:T(8,128)(2,1)}, u32[]{:S(2)}, u32[]{:S(2)}) async-start(bf16[16,16,2,16,128]{4,3,2,1,0:T(8,128)(2,1)} %filterbank.6), calls=%async_computation.2 | async-start | bytes 4194304 | tf_op jit(solution)/shard_map/all_to_all | solution.py:327
  135.0 52.4 %all-to-all-start = ((bf16[16,16,2,16,128]{4,3,2,1,0:T(8,128)(2,1)}), bf16[16,16,2,16,128]{4,3,2,1,0:T(8,128)(2,1)}, u32[]{:S(2)}, u32[]{:S(2)}) async-start(bf16[16,16,2,16,128]{4,3,2,1,0:T(8,128)(2,1)} %filterbank.4), calls=%async_computation | async-start | bytes 4194304 | tf_op jit(solution)/shard_map/all_to_all | solution.py:327
  157.5 34.8 %copy-start.1 = (s32[10]{0:T(128)S(1)}, s32[10]{0:T(128)}, u32[]{:S(2)}) copy-start(s32[10]{0:T(128)} %param.11) | copy-start | bytes 124
  187.4 52.4 %all-to-all-start.1 = ((bf16[16,16,2,16,128]{4,3,2,1,0:T(8,128)(2,1)}), bf16[16,16,2,16,128]{4,3,2,1,0:T(8,128)(2,1)}, u32[]{:S(2)}, u32[]{:S(2)}) async-start(bf16[16,16,2,16,128]{4,3,2,1,0:T(8,128)(2,1)} %filterbank.5), calls=%async_computation.1 | async-start | bytes 4194304 | tf_op jit(solution)/shard_map/all_to_all | solution.py:327

commit v3 on v2

--- a/solution.py
+++ b/solution.py
@@ -96,7 +96,6 @@
 LANES = 128
 CHUNK = 16
 PIECES = 4
-GROUPS = 1
 PRESCALE = 1024.0
 
 
@@ -122,9 +121,41 @@
 
 
 def filter_kernel(main, h0, h1, h2, taps, gain, weight, table, *rest):
-    groups = len(rest) - 2
-    outs, filt, turn = rest[:groups], rest[groups], rest[groups + 1]
-    sub = pl.program_id(0)
+    out, filt, turn, staged, send_sem, recv_sem, own_sem = rest
+    step = pl.program_id(0)
+    sub = lax.rem(step, 2)
+    piece = lax.div(step, 2)
+    me = lax.axis_index("wide")
+    devices = out.shape[1]
+    barrier = pltpu.get_barrier_semaphore()
+
+    @pl.when(step == 0)
+    def _():
+        @pl.loop(1, devices)
+        def _(o):
+            pl.semaphore_signal(
+                barrier,
+                inc=1,
+                device_id={"wide": lax.rem(me + o, devices)},
+                device_id_type=pl.DeviceIdType.MESH,
+            )
+
+        pl.semaphore_wait(barrier, devices - 1)
+
+    def remote(p, o, slot):
+        peer = lax.rem(me + o, devices)
+        return pltpu.make_async_remote_copy(
+            src_ref=staged.at[p, peer],
+            dst_ref=out.at[p, slot],
+            send_sem=send_sem.at[p, o],
+            recv_sem=recv_sem.at[p, o],
+            device_id={"wide": peer},
+            device_id_type=pl.DeviceIdType.MESH,
+        )
+
+    def own(p):
+        return pltpu.make_async_copy(staged.at[p, me], out.at[p, me], own_sem.at[p])
+
     inputs = main.shape[1]
     halos = (h0, h1, h2)
 
@@ -162,62 +193,78 @@
                     spectra[:, r * LANES : (r + 1) * LANES] * w
                 )
 
+    local = out.shape[2]
+
+    def stage(d):
+        rows = local * 2 * height
+        block = turn[pl.ds(pl.multiple_of(d * rows, rows), rows), :]
+        staged[piece, d] = block.astype(jnp.bfloat16).reshape(local, 2, height, LANES)
+
     @pl.when(sub == 1)
     def _():
-        dests, local, _, _, _ = outs[0].shape
-        every = local * groups
-
-        @pl.loop(0, dests)
-        def _(d):
-            for g in range(groups):
-                start = (d * every + g * local) * 2 * height
-                block = turn[pl.ds(pl.multiple_of(start, 2 * height), local * 2 * height), :]
-                outs[g][d] = block.astype(jnp.bfloat16).reshape(local, 2, height, LANES)
-
-
-def filter_piece(piece, turned, taps, gain, weight, table, dests):
+        @pl.loop(1, devices)
+        def _(o):
+            stage(lax.rem(me + o, devices))
+            remote(piece, o, me).start()
+
+        stage(me)
+        own(piece).start()
+
+    @pl.when(step == 2 * PIECES - 1)
+    def _():
+        @pl.loop(0, PIECES)
+        def _(p):
+            own(p).wait()
+
+            @pl.loop(1, devices)
+            def _(o):
+                remote(p, o, me).wait_send()
+                remote(p, o, lax.rem(me - o + devices, devices)).wait_recv()
+
+
+def filter_and_send(turned, taps, gain, weight, table, dests):
     _, inputs, samples = turned.shape
     channels = table.shape[0]
-    local = channels // 2 // dests // GROUPS
+    local = channels // 2 // dests
     height = 2 * CHUNK * inputs // LANES
-    shape = jax.ShapeDtypeStruct((dests, local, 2, height, LANES), jnp.bfloat16)
+    shape = (PIECES, dests, local, 2, height, LANES)
     halo = [
-        pl.BlockSpec((1, inputs, samples), lambda i, j=j: ((piece * 2 + i + 1) * CHUNK + j, 0, 0))
+        pl.BlockSpec((1, inputs, samples), lambda i, j=j: ((i + 1) * CHUNK + j, 0, 0))
         for j in range(3)
     ]
     whole = lambda x: pl.BlockSpec(x.shape, lambda i: (0, 0))
     return pl.pallas_call(
         filter_kernel,
-        grid=(2,),
-        in_specs=[pl.BlockSpec((CHUNK, inputs, samples), lambda i: (piece * 2 + i, 0, 0))]
+        grid=(2 * PIECES,),
+        in_specs=[pl.BlockSpec((CHUNK, inputs, samples), lambda i: (i, 0, 0))]
         + halo
         + [whole(taps), whole(gain), whole(weight), whole(table)],
-        out_specs=[pl.BlockSpec(shape.shape, lambda i: (0, 0, 0, 0, 0))] * GROUPS,
-        out_shape=[shape] * GROUPS,
+        out_specs=pl.BlockSpec(memory_space=pl.ANY),
+        out_shape=jax.ShapeDtypeStruct(shape, jnp.bfloat16),
         scratch_shapes=[
             pltpu.VMEM((CHUNK * inputs, samples), jnp.bfloat16),
             pltpu.VMEM((channels * height, LANES), jnp.float32),
+            pltpu.VMEM(shape, jnp.bfloat16),
+            pltpu.SemaphoreType.DMA((PIECES, dests)),
+            pltpu.SemaphoreType.DMA((PIECES, dests)),
+            pltpu.SemaphoreType.DMA((PIECES,)),
         ],
-        compiler_params=pltpu.CompilerParams(vmem_limit_bytes=52 * 2**20),
-        cost_estimate=pl.CostEstimate(
-            flops=2 * 2 * CHUNK * inputs * samples * channels,
-            bytes_accessed=2 * (CHUNK + 3) * inputs * samples * 2 + 6 * 2**20,
-            transcendentals=0,
+        compiler_params=pltpu.CompilerParams(
+            vmem_limit_bytes=56 * 2**20, collective_id=0, has_side_effects=True
         ),
-        name="filterbank",
+        name="filterbank_send",
     )(turned, turned, turned, turned, taps, gain, weight, table)
 
 
 def correlate_kernel(slots, *rest, block, frames):
-    pieces = rest[: PIECES]
-    out, stacked, rotated, flipped = rest[PIECES:]
-    sources, _, _, height, _ = pieces[0].shape
+    received, out, stacked, rotated, flipped = rest
+    _, sources, _, _, height, _ = received.shape
     half = LANES // 2
     for p in range(PIECES):
         for part in range(2):
             for s in range(0, sources, 2):
-                first = pieces[p][s, 0, part]
-                second = pieces[p][s + 1, 0, part]
+                first = received[p, s, 0, part]
+                second = received[p, s + 1, 0, part]
                 row = part * frames + p * 2 * height
                 cols = slice(s * half, s * half + LANES)
                 stacked[row : row + height, cols] = jnp.concatenate(
@@ -248,29 +295,24 @@
                 out[0, slot, part] = (gram * scale).astype(jnp.bfloat16)
 
 
-def correlate(slots, pieces, offset, total, previous):
-    sources, local, _, height, _ = pieces[0].shape
+def correlate(slots, received):
+    _, sources, local, _, height, _ = received.shape
     inputs = sources * LANES // 2
     frames = PIECES * height * 2
     tiles = slots.shape[0]
-    in_specs = [pl.BlockSpec((sources, 1, 2, height, LANES), lambda k, *_: (0, k, 0, 0, 0))] * PIECES
-    operands = [slots, *pieces]
     kernel = functools.partial(correlate_kernel, block=BLK, frames=frames)
-    aliases = {}
-    if previous is not None:
-        base = kernel
-        kernel = lambda s, prev, *rest: base(s, *rest)
-        in_specs = [pl.BlockSpec(memory_space=pl.ANY)] + in_specs
-        operands = [slots, previous, *pieces]
-        aliases = {1: 0}
     return pl.pallas_call(
         kernel,
         grid_spec=pltpu.PrefetchScalarGridSpec(
             num_scalar_prefetch=1,
             grid=(local,),
-            in_specs=in_specs,
+            in_specs=[
+                pl.BlockSpec(
+                    (PIECES, sources, 1, 2, height, LANES), lambda k, *_: (0, 0, k, 0, 0, 0)
+                )
+            ],
             out_specs=pl.BlockSpec(
-                (1, tiles, 2, BLK, BLK), lambda k, *_: (k + offset, 0, 0, 0, 0)
+                (1, tiles, 2, BLK, BLK), lambda k, *_: (k, 0, 0, 0, 0)
             ),
             scratch_shapes=[
                 pltpu.VMEM((2 * frames, inputs), jnp.bfloat16),
@@ -278,8 +320,7 @@
                 pltpu.VMEM((inputs, 2 * frames), jnp.bfloat16),
             ],
         ),
-        out_shape=jax.ShapeDtypeStruct((total, tiles, 2, BLK, BLK), jnp.bfloat16),
-        input_output_aliases=aliases,
+        out_shape=jax.ShapeDtypeStruct((local, tiles, 2, BLK, BLK), jnp.bfloat16),
         compiler_params=pltpu.CompilerParams(vmem_limit_bytes=40 * 2**20),
         cost_estimate=pl.CostEstimate(
             flops=local * tiles * 2 * 2 * BLK * BLK * 2 * frames,
@@ -287,7 +328,7 @@
             transcendentals=0,
         ),
         name="correlate",
-    )(*operands)
+    )(slots, received)
 
 
 def body(voltages, filter_taps, input_gain, input_flags, kept_channels, tile_order):
@@ -301,7 +342,7 @@
         and taps == 4
         and frames == PIECES * 2 * CHUNK
         and devices % 2 == 0
-        and kept % (devices * GROUPS) == 0
+        and kept % devices == 0
         and samples % LANES == 0
     )
     if not fits:
@@ -319,18 +360,8 @@
     slots = jnp.sum(
         jnp.where(tile_order[None, :] == numbers[:, None], numbers[None, :], 0), axis=1
     ).astype(jnp.int32)
-    received = [[] for _ in range(GROUPS)]
-    for piece in range(PIECES):
-        outs = filter_piece(piece, turned, float_taps, gain, weight, table, devices)
-        for g in range(GROUPS):
-            received[g].append(
-                lax.all_to_all(outs[g], "wide", split_axis=0, concat_axis=0, tiled=True)
-            )
-    local = kept // devices
-    result = None
-    for g in range(GROUPS):
-        result = correlate(slots, received[g], g * (local // GROUPS), local, result)
-    return result
+    received = filter_and_send(turned, float_taps, gain, weight, table, devices)
+    return correlate(slots, received)
 
 
 def solution(mesh):

time: 268 us -> 247 us (0.922)
  waiting for transfers between devices: 137 us -> 0 us
  Pallas kernels: 97.6 us -> 229 us
  starting transfers between devices: 21.3 us -> 0 us
  local copies, waits for them, and re-layouts: 4.48 us -> 9.11 us
    all_to_all x4 -> x0, waiting for transfers between devices: 137 us -> none  [body(): lax.all_to_all(outs[g], 'wide', split_axis=0, concat_axis=0, tiled=True)]
    pallas_call x4 -> x1, Pallas kernels: 70.2 us -> 202 us  [filter_and_send(): pl.pallas_call(filter_kernel, grid=(2 * PIECES,), in_specs=[pl.BlockSpec(...]
    all_to_all x4 -> x0, starting transfers between devices: 21.3 us -> none  [body(): lax.all_to_all(outs[g], 'wide', split_axis=0, concat_axis=0, tiled=True)]
    unnamed x4 -> x2, local copies, waits for them, and re-layouts: 0.01 us -> 3.37 us
  transfers between devices with their start and end apart: 4 -> 0, of which waited for: 4 -> 0; matrix products, arithmetic and copies ran while one was open for 0% -> 0% of each run, Pallas kernels for 20% -> 0%
where the time goes in v3:
time: 247 us
  Pallas kernels  229 us (93%)
  local copies, waits for them, and re-layouts  9.11 us (4%)
  other arithmetic  8.28 us (3%)
    pallas_call x1, Pallas kernels, filter_and_send(): pl.pallas_call(filter_kernel, grid=(2 * PIECES,), in_specs=[pl.BlockSpec(...  202 us
    pallas_call x1, Pallas kernels, correlate(): pl.pallas_call(kernel, grid_spec=pltpu.PrefetchScalarGridSpec(num_scalar_...  26.7 us

profile of v3, /device:TPU:15, one launch (start us, length us, event | category | flops | bytes accessed | tf_op | source)
XLA Modules:
  0.0 246.6 jit_solution(3461808623845769542)
XLA Ops:
  0.0 0.7 convert_multiply_fusion
  0.7 0.6 maximum_bitcast_fusion.weight
  1.2 0.8 select_reduce_fusion.slots
  2.0 0.8 sine_multiply_fusion
  2.8 1.3 convert_element_type.15.taps
  4.2 1.3 broadcast_in_dim.14.gain
  5.5 1.3 fusion.6
  6.8 0.1 constant_dynamic-update-slice_fusion.15
  7.0 0.2 constant_dynamic-update-slice_fusion.14
  7.2 0.2 constant_dynamic-update-slice_fusion.13
  7.3 0.2 constant_dynamic-update-slice_fusion.12
  7.5 0.2 constant_dynamic-update-slice_fusion.11
  7.7 0.2 constant_dynamic-update-slice_fusion.10
  7.9 0.2 constant_dynamic-update-slice_fusion.9
  8.0 0.2 constant_dynamic-update-slice_fusion.8
  8.2 0.2 constant_dynamic-update-slice_fusion.7
  8.4 0.2 constant_dynamic-update-slice_fusion.6
  8.6 0.2 constant_dynamic-update-slice_fusion.5
  8.7 0.2 constant_dynamic-update-slice_fusion.4
  8.9 0.2 constant_dynamic-update-slice_fusion.3
  9.1 0.2 constant_dynamic-update-slice_fusion.2
  9.3 0.2 constant_dynamic-update-slice_fusion.1
  9.4 0.2 constant_dynamic-update-slice_fusion
  9.6 0.2 pad_maximum_fusion
  9.8 2.2 copy.9
  12.0 2.2 convert_element_type.19.table
  14.2 202.3 %filterbank_send.1.rest_0_ = bf16[4,16,16,2,16,128]{5,4,3,2,1,0:T(8,128)(2,1)} custom-call(bf16[131,64,2048]{2,1,0:T(8,128)(2,1)} %bitcast.37, bf16[131,64,2048]{2,1,0:T(8,128)(2,1)} %bitcast.38, bf16[131,64,2048]{2,1,0:T(8,128)(2,1)} %bitcast.39, bf16[131,64,2048]{2,1,0:T(8,128)(2,1)} %bitcast.40, f32[4,2048]{1,0:T(4,128)} %convert_element_type.15.taps, ...), custom_call_target="tpu_custom_call" | custom-call | tf_op jit(solution)/shard_map/filterbank_send/pallas_call | solution.py:236
  216.5 0.0 copy-start
  216.5 3.4 %copy-done = bf16[4,16,16,2,16,128]{5,4,3,2,1,0:T(8,128)(2,1)S(1)} copy-done((bf16[4,16,16,2,16,128]{5,4,3,2,1,0:T(8,128)(2,1)S(1)}, bf16[4,16,16,2,16,128]{5,4,3,2,1,0:T(8,128)(2,1)}, u32[]{:S(2)}) %copy-start) | copy-done | bytes 8388632
  219.9 26.7 %correlate.1 = bf16[16,10,2,256,256]{4,3,2,1,0:T(8,128)(2,1)} custom-call(s32[10]{0:T(128)S(1)} %select_reduce_fusion.slots, bf16[4,16,16,2,16,128]{5,4,3,2,1,0:T(8,128)(2,1)S(1)} %copy-done), custom_call_target="tpu_custom_call" | custom-call | flops 10737418240 | bytes 50331648 | tf_op jit(solution)/shard_map/correlate/pallas_call | solution.py:304
  (3 shorter events, 0.0 us)
Async XLA Ops:
  216.5 3.4 %copy-start = (bf16[4,16,16,2,16,128]{5,4,3,2,1,0:T(8,128)(2,1)S(1)}, bf16[4,16,16,2,16,128]{5,4,3,2,1,0:T(8,128)(2,1)}, u32[]{:S(2)}) copy-start(bf16[4,16,16,2,16,128]{5,4,3,2,1,0:T(8,128)(2,1)} %filterbank_send.1.rest_0_) | copy-start | bytes 25165828

commit v4 on v3

--- a/solution.py
+++ b/solution.py
@@ -203,7 +203,8 @@
     @pl.when(sub == 1)
     def _():
         @pl.loop(1, devices)
-        def _(o):
+        def _(k):
+            o = lax.rem(k + devices // 2 - 2, devices - 1) + 1
             stage(lax.rem(me + o, devices))
             remote(piece, o, me).start()
 
@@ -321,7 +322,7 @@
             ],
         ),
         out_shape=jax.ShapeDtypeStruct((local, tiles, 2, BLK, BLK), jnp.bfloat16),
-        compiler_params=pltpu.CompilerParams(vmem_limit_bytes=40 * 2**20),
+        compiler_params=pltpu.CompilerParams(vmem_limit_bytes=60 * 2**20),
         cost_estimate=pl.CostEstimate(
             flops=local * tiles * 2 * 2 * BLK * BLK * 2 * frames,
             bytes_accessed=local * (tiles * 2 * BLK * BLK * 2 + inputs * frames * 4),

time: 247 us -> 247 us (level)
  local copies, waits for them, and re-layouts: 9.11 us -> 5.73 us
    unnamed x2 -> x0, local copies, waits for them, and re-layouts: 3.37 us -> none
where the time goes in v4:
time: 247 us; the launch traced here: 244 us
  Pallas kernels  229 us (93%)
  other arithmetic  8.84 us (4%)
  local copies, waits for them, and re-layouts  5.73 us (2%)
    pallas_call x1, Pallas kernels, filter_and_send(): pl.pallas_call(filter_kernel, grid=(2 * PIECES,), in_specs=[pl.BlockSpec(...  202 us
    pallas_call x1, Pallas kernels, correlate(): pl.pallas_call(kernel, grid_spec=pltpu.PrefetchScalarGridSpec(num_scalar_...  27.2 us

profile of v4, /device:TPU:15, one launch (start us, length us, event | category | flops | bytes accessed | tf_op | source)
XLA Modules:
  0.0 244.2 jit_solution(5886916219761369188)
XLA Ops:
  0.0 0.7 convert_multiply_fusion
  0.7 0.6 maximum_bitcast_fusion.weight
  1.2 1.3 select_reduce_fusion.slots
  2.6 0.8 sine_multiply_fusion
  3.4 1.3 convert_element_type.15.taps
  4.7 1.3 broadcast_in_dim.14.gain
  6.1 1.3 fusion.6
  7.4 0.1 constant_dynamic-update-slice_fusion.15
  7.5 0.2 constant_dynamic-update-slice_fusion.14
  7.7 0.2 constant_dynamic-update-slice_fusion.13
  7.9 0.2 constant_dynamic-update-slice_fusion.12
  8.1 0.2 constant_dynamic-update-slice_fusion.11
  8.2 0.2 constant_dynamic-update-slice_fusion.10
  8.4 0.2 constant_dynamic-update-slice_fusion.9
  8.6 0.2 constant_dynamic-update-slice_fusion.8
  8.8 0.2 constant_dynamic-update-slice_fusion.7
  8.9 0.2 constant_dynamic-update-slice_fusion.6
  9.1 0.2 constant_dynamic-update-slice_fusion.5
  9.3 0.2 constant_dynamic-update-slice_fusion.4
  9.5 0.2 constant_dynamic-update-slice_fusion.3
  9.6 0.2 constant_dynamic-update-slice_fusion.2
  9.8 0.2 constant_dynamic-update-slice_fusion.1
  10.0 0.2 constant_dynamic-update-slice_fusion
  10.2 0.2 pad_maximum_fusion
  10.4 2.2 copy.9
  12.5 2.2 convert_element_type.19.table
  14.7 202.3 %filterbank_send.1.rest_0_ = bf16[4,16,16,2,16,128]{5,4,3,2,1,0:T(8,128)(2,1)} custom-call(bf16[131,64,2048]{2,1,0:T(8,128)(2,1)} %bitcast.37, bf16[131,64,2048]{2,1,0:T(8,128)(2,1)} %bitcast.38, bf16[131,64,2048]{2,1,0:T(8,128)(2,1)} %bitcast.39, bf16[131,64,2048]{2,1,0:T(8,128)(2,1)} %bitcast.40, f32[4,2048]{1,0:T(4,128)} %convert_element_type.15.taps, ...), custom_call_target="tpu_custom_call" | custom-call | tf_op jit(solution)/shard_map/filterbank_send/pallas_call | solution.py:237
  217.0 27.2 %correlate.1 = bf16[16,10,2,256,256]{4,3,2,1,0:T(8,128)(2,1)} custom-call(s32[10]{0:T(128)} %select_reduce_fusion.slots, bf16[4,16,16,2,16,128]{5,4,3,2,1,0:T(8,128)(2,1)} %filterbank_send.1.rest_0_), custom_call_target="tpu_custom_call" | custom-call | flops 10737418240 | bytes 50331648 | tf_op jit(solution)/shard_map/correlate/pallas_call | solution.py:305
  (3 shorter events, 0.0 us)
